TPU v7x, 256 devices: a whole 4x4x8 slice. The times are simulated.
256 devices in a mesh: grp: 8 (over y, core), cand: 32 (over z, x).
Axes of the slice: x: 4, y: 4, z: 8, core: 2. Of those that a mesh axis runs over, the one named last changes fastest.
Arguments:
- history: bfloat16 [32, 512, 256], P('grp', 'cand'), parts along dimension 0, may hold values from -6 to 6
- cands: bfloat16 [32, 8192, 256], P('grp', 'cand'), parts along dimension 0, may hold values from -400 to 400, as said below
- surv_count: int32 [32, 32], P('grp', 'cand'), parts along dimension 0, may hold values from 1 to 256, 4096 in all within a row
- surv_index: int32 [32, 8192], P('grp', 'cand'), parts along dimension 0, may hold values from 0 to 255
- pre_wq: bfloat16 [256, 256], replicated, may hold values from -0.375 to 0.375
- pre_wkv: bfloat16 [256, 512], replicated, may hold values from -0.375 to 0.375
- rank_wq: bfloat16 [256, 1024], replicated, may hold values from -0.375 to 0.375
- rank_wkv: bfloat16 [256, 2048], replicated, may hold values from -0.375 to 0.375
- norm_gain: float32 [1024], replicated, may hold values from 0.1 to 1.9
- mlp_up: bfloat16 [1024, 4096], replicated, may hold values from -0.1875 to 0.1875
- score_w: bfloat16 [4096], replicated, may hold values from -0.09375 to 0.09375
Outputs:
- pre_score: float32 [32, 8192], P('grp', 'cand'), parts along dimension 0
- rank_score: float32 [32, 8192], P('grp', 'cand'), parts along dimension 0
There are 8 independent parts, one for each index of `grp`. A program takes and returns all parts, laid end to end along the dimension named above; an argument that names none is the same for every part. Nothing has to cross between parts.
Inputs may be any that keep to these rules, and one draw needn't show every extreme that they name: `cands`: feature values of candidates lie within the stated range.
All inputs are finite; a program needn't handle non-finite values. No bound on the sum of `surv_count` on one device may be relied on, other than what follows from the above.
Results may differ from a plain program's by a relative error of at most 0.01.
The roundings to bfloat16 on the way count: a program that leaves them out, or rounds other values in their place, can miss the bound.
Values may be sent and summed in bfloat16 or wider, within the bound.
No kernel may reach another device: no remote copies, remote signals or barrier semaphores. Data moves between devices by JAX's collectives and lax.ppermute only.
A program may use at most 128 MiB of HBM per device.

v0:
```python
import functools
import math

import jax
import jax.numpy as jnp
from jax import lax
from jax.experimental import pallas as pl
from jax.experimental.pallas import tpu as pltpu
from jax.sharding import PartitionSpec as P

HEADS = 8
BF = jnp.bfloat16
F32 = jnp.float32
I32 = jnp.int32
LOG2E = 1.4426950408889634
GELU_A = math.sqrt(2.0 / math.pi)
GELU_B = GELU_A * 0.044715
ROW_TILES = (128, 176, 256)
MLP_ROWS = (128, 192, 256, 352)
MLP_COLS = 512
PRE_Q = 1024
PRE_WKV = 1280
RANK_WK = 1536
RANK_WV = 1792
SMALL = 2048
PACK = 2064
FIXED = PRE_Q
SELECT_LIMIT = 57 * 2**20
RANK_LIMIT = 50 * 2**20
STAGE_LIMIT = 50 * 2**20
VMEM = pl.BlockSpec(memory_space=pltpu.VMEM)
SMEM = pl.BlockSpec(memory_space=pltpu.SMEM)
HBM = pl.BlockSpec(memory_space=pltpu.HBM)


def dot(a, b):
    return jnp.dot(a, b, preferred_element_type=F32)


def dot_t(a, b):
    return lax.dot_general(a, b, (((1,), (1,)), ((), ())), preferred_element_type=F32)


def select_kernel(
    count_ref,
    index_ref,
    cands_hbm,
    wq_hbm,
    pre_wq_hbm,
    pre_wkv_hbm,
    wkv_hbm,
    gain_ref,
    score_w_ref,
    pack_hbm,
    pack_ref,
    cands_ref,
    wq_ref,
    pre_wq_ref,
    sems,
    out_sem,
):
    width = pack_hbm.shape[1]
    pairs = (
        (cands_hbm, cands_ref),
        (wq_hbm, wq_ref),
        (pre_wq_hbm, pre_wq_ref),
        (pre_wkv_hbm, pack_ref.at[pl.ds(PRE_WKV, pre_wkv_hbm.shape[0]), pl.ds(0, pre_wkv_hbm.shape[1])]),
        (wkv_hbm.at[:, pl.ds(0, width)], pack_ref.at[pl.ds(RANK_WK, RANK_WV - RANK_WK)]),
        (wkv_hbm.at[:, pl.ds(width, width)], pack_ref.at[pl.ds(RANK_WV, SMALL - RANK_WV)]),
    )
    copies = [pltpu.make_async_copy(a, b, sems.at[i]) for i, (a, b) in enumerate(pairs)]
    for copy in copies:
        copy.start()
    requests, slots = index_ref.shape
    _, cands, features = cands_ref.shape
    row_c = lax.broadcasted_iota(I32, (cands, slots), 0)
    lane = lax.broadcasted_iota(I32, (1, slots), 1)
    before = (
        lax.broadcasted_iota(I32, (cands, cands), 0) < lax.broadcasted_iota(I32, (cands, cands), 1)
    ).astype(BF)
    place_c = lax.broadcasted_iota(I32, (slots, cands), 0).astype(F32)
    ones = jnp.ones((8, slots), BF)
    for copy in copies[:3]:
        copy.wait()
    start = jnp.int32(0)
    places = []
    for r in range(requests):
        valid = lane < count_ref[r]
        picked = jnp.where(valid, index_ref[r : r + 1, :], -1)
        match = (row_c == picked).astype(F32).astype(BF)
        used = jnp.where(dot_t(ones, match) > 0.5, 1.0, 0.0)
        position = dot(used.astype(BF), before)
        number = jnp.sum(used[0:1, :]).astype(I32)
        places.append(jnp.where(valid, dot(position.astype(BF), match)[0:1, :], -1.0))
        chosen = jnp.where((used[0:1, :] > 0.5) & (position[0:1, :] == place_c), 1.0, 0.0).astype(BF)
        mine = cands_ref[r]
        rows = dot(chosen, mine).astype(BF)
        pack_ref[pl.ds(pl.multiple_of(start, 16), slots), :] = dot(rows, wq_ref[...]).astype(BF)
        start = start + (((number + 15) >> 4) << 4)
        pack_ref[PRE_Q : PRE_Q + features, r * slots : (r + 1) * slots] = lax.dot_general(
            pre_wq_ref[...], mine, (((0,), (1,)), ((), ())), preferred_element_type=F32
        ).astype(BF)
    gain = gain_ref[...]
    high = gain.astype(BF).astype(F32)
    middle = (gain - high).astype(BF).astype(F32)
    per_row = width // 128
    small = [jnp.concatenate(places, axis=1), high, middle, gain - high - middle]
    for k in range(score_w_ref.shape[0] // per_row):
        lanes = [score_w_ref[i : i + 1, :].astype(F32) for i in range(k * per_row, (k + 1) * per_row)]
        small.append(jnp.concatenate(lanes, axis=1))
    small.append(jnp.zeros((PACK - SMALL - len(small), width), F32))
    pack_ref[SMALL:PACK, :] = jnp.concatenate(small, axis=0).astype(BF)
    for copy in copies[3:]:
        copy.wait()
    write = pltpu.make_async_copy(pack_ref, pack_hbm, out_sem)
    write.start()
    write.wait()


def attend(
    chunk_refs,
    pack_hbm,
    fixed_ref,
    query_ref,
    query_sem,
    keys_ref,
    values_ref,
    normed_ref,
    pre_out,
    up_copy,
):
    requests, slots = pre_out.shape
    events, width = keys_ref.shape
    half = width // 2
    head = width // HEADS
    features = chunk_refs[0].shape[-1]
    query_copy = pltpu.make_async_copy(pack_hbm.at[pl.ds(0, PRE_Q)], query_ref, query_sem)
    query_copy.start()
    up_copy.start()
    for h in range(HEADS):
        values_ref[:, (2 * h + 1) * head : (2 * h + 2) * head] = jnp.ones((events, head), BF)
    scale = LOG2E / math.sqrt(head)
    pre_w = slice(PRE_WKV - FIXED, PRE_WKV - FIXED + features)
    pre_scale = LOG2E / math.sqrt(features)
    small = fixed_ref[SMALL - FIXED : PACK - FIXED, :].astype(F32)
    gain = small[1:2, :] + small[2:3, :] + small[3:4, :]
    numbers = [jnp.max(small[0:1, r * slots : (r + 1) * slots]).astype(I32) + 1 for r in range(requests)]
    starts = [jnp.int32(0)]
    for number in numbers:
        starts.append(starts[-1] + (((number + 15) >> 4) << 4))

    def request(r, carry):
        number, start = numbers[0], starts[0]
        for k in range(1, requests):
            number, start = jnp.where(r == k, numbers[k], number), jnp.where(r == k, starts[k], start)
        parts = [ref[:, pl.ds(r, 1)].reshape(events // len(chunk_refs), features) for ref in chunk_refs]
        history = jnp.concatenate(parts, axis=0)

        def put_keys(c):
            cols = slice(c * half, (c + 1) * half)
            keys_ref[:, cols] = dot(history, fixed_ref[RANK_WK - FIXED : RANK_WV - FIXED, cols]).astype(BF)

        def put_values(c):
            part = dot(history, fixed_ref[RANK_WV - FIXED : SMALL - FIXED, c * half : (c + 1) * half]).astype(BF)
            for k in range(HEADS // 2):
                h = c * HEADS // 2 + k
                values_ref[:, 2 * h * head : (2 * h + 1) * head] = part[:, k * head : (k + 1) * head]

        pre_q = fixed_ref[PRE_Q - FIXED : PRE_Q - FIXED + features, pl.ds(pl.multiple_of(r * slots, slots), slots)]
        pre_keys = dot(history, fixed_ref[pre_w, :features]).astype(BF)
        pre_values = lax.dot_general(
            fixed_ref[pre_w, features : 2 * features],
            history,
            (((0,), (1,)), ((), ())),
            preferred_element_type=F32,
        ).astype(BF)
        put_keys(0)
        logits = dot(pre_keys, pre_q)
        put_keys(1)
        top = jnp.max(logits, axis=0, keepdims=True)
        weights = jnp.exp2((logits - top) * pre_scale)
        weights = (weights * (1.0 / jnp.sum(weights, axis=0, keepdims=True))).astype(BF)
        put_values(0)
        pooled = dot(pre_values, weights)
        put_values(1)
        query = pre_q.astype(F32)
        length = jnp.sqrt(jnp.sum(query * query, axis=0, keepdims=True))
        pre_out[pl.ds(r, 1), :] = jnp.sum(pooled * query, axis=0, keepdims=True) / (1.0 + length)
        pl.when(r == 0)(query_copy.wait)

        def tile(rows):
            at = pl.ds(pl.multiple_of(start, 16), rows)
            mixed = []
            for h in range(HEADS):
                cols = slice(h * head, (h + 1) * head)
                query = query_ref[at, cols]
                logits = dot_t(query, keys_ref[:, cols])
                top = jnp.max(logits, axis=1, keepdims=True)
                weights = jnp.exp2((logits - top) * scale).astype(BF)
                both = dot(weights, values_ref[:, 2 * h * head : (2 * h + 2) * head])
                mixed.append(query.astype(F32) + both[:, :head] / both[:, head:])
            acc = mixed[0]
            for one in mixed[1:]:
                acc = acc + one
            center = jnp.sum(acc, axis=1, keepdims=True) * (1.0 / width)
            acc = jnp.zeros((rows, head), F32)
            for one in mixed:
                acc = acc + (one - center) * (one - center)
            spread = jnp.sum(acc, axis=1, keepdims=True) * (1.0 / width)
            inverse = lax.rsqrt(spread + 1e-05)
            for h in range(HEADS):
                cols = slice(h * head, (h + 1) * head)
                normed_ref[at, cols] = ((mixed[h] - center) * inverse * gain[:, cols]).astype(BF)

        low = 0
        for rows in ROW_TILES:
            pl.when((number > low) & (number <= rows))(functools.partial(tile, rows))
            low = rows
        return carry

    lax.fori_loop(0, requests, request, 0)
    return starts, small


def rank_kernel(
    own_ref, a_ref, b_ref, c_ref, pack_hbm, fixed_ref, up_hbm,
    pre_out, rank_out,
    keys_ref, values_ref, query_ref, query_sem, normed_ref, ranked_ref, up_ref, sem,
):
    up_copy = pltpu.make_async_copy(up_hbm, up_ref, sem)
    requests, slots = rank_out.shape
    starts, small = attend(
        (own_ref, a_ref, b_ref, c_ref), pack_hbm, fixed_ref, query_ref, query_sem, keys_ref, values_ref, normed_ref,
        pre_out, up_copy,
    )
    up_copy.wait()
    width, hidden_size = up_ref.shape

    def mlp(first, count):
        at = pl.ds(pl.multiple_of(first, 16), count)
        rows = normed_ref[at, :]
        acc = jnp.zeros((count, 128), F32)
        for j in range(hidden_size // MLP_COLS):
            cols = slice(j * MLP_COLS, (j + 1) * MLP_COLS)
            x = dot(rows, up_ref[:, cols])
            x = x + x * jnp.tanh(x * (GELU_A + GELU_B * (x * x)))
            for k in range(MLP_COLS // 128):
                row, lane = divmod(j * MLP_COLS + k * 128, width)
                weight = 0.5 * small[4 + row : 5 + row, lane : lane + 128]
                acc = acc + x[:, k * 128 : (k + 1) * 128] * weight
        ranked_ref[at, :] = jnp.broadcast_to(jnp.sum(acc, axis=1, keepdims=True), acc.shape)

    def step(t, carry):
        first = t * MLP_ROWS[-1]
        left = starts[requests] - first
        low = 0
        for count in MLP_ROWS:
            high = count if count < MLP_ROWS[-1] else requests * slots
            pl.when((left > low) & (left <= high))(functools.partial(mlp, first, count))
            low = count
        return carry

    lax.fori_loop(0, (starts[requests] + MLP_ROWS[-1] - 1) // MLP_ROWS[-1], step, 0)
    row = lax.broadcasted_iota(I32, (slots, slots), 0).astype(F32)
    for r in range(requests):
        ranked = ranked_ref[pl.ds(pl.multiple_of(starts[r], 16), slots), :]
        ranked = jnp.concatenate([ranked] * (slots // 128), axis=1)
        hit = row == small[0:1, r * slots : (r + 1) * slots]
        rank_out[r : r + 1, :] = jnp.sum(jnp.where(hit, ranked, 0.0), axis=0, keepdims=True)


def select_call(surv_count, surv_index, cands, rank_wq, pre_wq, pre_wkv, rank_wkv, norm_gain, score_w):
    requests, slots = surv_index.shape
    width = rank_wq.shape[1]
    return pl.pallas_call(
        select_kernel,
        name="select",
        out_shape=jax.ShapeDtypeStruct((PACK, width), BF),
        in_specs=[SMEM, VMEM, HBM, HBM, HBM, HBM, HBM, VMEM, VMEM],
        out_specs=HBM,
        scratch_shapes=[
            pltpu.VMEM((PACK, width), BF),
            pltpu.VMEM(cands.shape, BF),
            pltpu.VMEM(rank_wq.shape, BF),
            pltpu.VMEM(pre_wq.shape, BF),
            pltpu.SemaphoreType.DMA((6,)),
            pltpu.SemaphoreType.DMA,
        ],
        compiler_params=pltpu.CompilerParams(vmem_limit_bytes=SELECT_LIMIT),
        cost_estimate=pl.CostEstimate(flops=2 * 10**9, bytes_accessed=12 * 2**20, transcendentals=0),
    )(
        surv_count.reshape(requests), surv_index, cands, rank_wq, pre_wq, pre_wkv, rank_wkv,
        norm_gain.reshape(1, -1), score_w.reshape(-1, 128),
    )


def stage_kernel(pack_hbm, fixed_ref, sem):
    copy = pltpu.make_async_copy(pack_hbm.at[pl.ds(FIXED, PACK - FIXED)], fixed_ref, sem)
    copy.start()
    copy.wait()


def stage_call(pack):
    return pl.pallas_call(
        stage_kernel,
        name="stage",
        out_shape=jax.ShapeDtypeStruct((PACK - FIXED, pack.shape[1]), BF),
        in_specs=[HBM],
        out_specs=VMEM,
        scratch_shapes=[pltpu.SemaphoreType.DMA],
        compiler_params=pltpu.CompilerParams(vmem_limit_bytes=STAGE_LIMIT),
        cost_estimate=pl.CostEstimate(flops=0, bytes_accessed=4 * 2**20, transcendentals=0),
    )(pack)


def rank_call(chunks, pack, fixed, mlp_up):
    nz, requests, here, _ = chunks[0].shape
    width = pack.shape[1]
    slots = width // requests
    events = len(chunks) * nz * here
    padded = -(-requests * slots // MLP_ROWS[-1]) * MLP_ROWS[-1]
    score = jax.ShapeDtypeStruct((requests, slots), F32)
    return pl.pallas_call(
        rank_kernel,
        name="rank",
        out_shape=(score, score),
        in_specs=[VMEM] * 4 + [HBM, VMEM, HBM],
        out_specs=(VMEM, VMEM),
        scratch_shapes=[
            pltpu.VMEM((events, width), BF),
            pltpu.VMEM((events, 2 * width), BF),
            pltpu.VMEM((PRE_Q, width), BF),
            pltpu.SemaphoreType.DMA,
            pltpu.VMEM((padded, width), BF),
            pltpu.VMEM((padded, 128), F32),
            pltpu.VMEM(mlp_up.shape, BF),
            pltpu.SemaphoreType.DMA,
        ],
        compiler_params=pltpu.CompilerParams(vmem_limit_bytes=RANK_LIMIT),
        cost_estimate=pl.CostEstimate(flops=16 * 10**9, bytes_accessed=20 * 2**20, transcendentals=4 * 10**6),
    )(*chunks, pack, fixed, mlp_up)


def body(history, cands, surv_count, surv_index, pre_wq, pre_wkv, rank_wq, rank_wkv, norm_gain, mlp_up, score_w):
    nx = 4
    nz = lax.axis_size("cand") // nx
    columns = [[z * nx + x for z in range(nz)] for x in range(nx)]

    def shift(x, by):
        pairs = [(z * nx + a, z * nx + (a + by) % nx) for z in range(nz) for a in range(nx)]
        return lax.ppermute(x, "cand", pairs)

    copies = jnp.broadcast_to(history[None], (nz,) + history.shape)
    own = lax.all_to_all(copies, "cand", split_axis=0, concat_axis=0, tiled=True, axis_index_groups=columns)
    pack = select_call(
        surv_count, surv_index, cands, rank_wq, pre_wq, pre_wkv, rank_wkv, norm_gain, score_w
    )
    chunks = [own] + [shift(own, by) for by in (1, 3, 2)]
    return rank_call(chunks, pack, stage_call(pack), mlp_up)


def solution(mesh):
    in_specs = (
        P("grp", "cand", None),
        P("grp", "cand", None),
        P("grp", "cand"),
        P("grp", "cand"),
        P(),
        P(),
        P(),
        P(),
        P(),
        P(),
        P(),
    )
    out_specs = (P("grp", "cand"), P("grp", "cand"))
    return jax.shard_map(body, mesh=mesh, in_specs=in_specs, out_specs=out_specs, check_vma=False)
```

profile of v0, /device:TPU:30, one launch (start us, length us, event | category | flops | bytes accessed | tf_op | source)
XLA Modules:
  0.0 53.9 jit_solution(14026340159326523594)
XLA Ops:
  0.6 0.8 %broadcast_in_dim.2 = bf16[8,4,16,256]{3,2,1,0:T(8,128)(2,1)S(1)} broadcast(bf16[4,16,256]{2,1,0:T(8,128)(2,1)} %param.11), dimensions={1,2,3} | broadcast | bytes 294912 | tf_op jit(solution)/shard_map/broadcast_in_dim | solution.py:353
  1.4 20.1 %all_to_all.5.own_ref = bf16[8,4,16,256]{3,2,1,0:T(8,128)(2,1)S(1)} all-to-all(bf16[8,4,16,256]{3,2,1,0:T(8,128)(2,1)S(1)} %broadcast_in_dim.2), channel_id=1, replica_groups={{0,4,8,12,16,20,24,28},{1,5,9,13,17,21,25,29},{2,6,10,14,18,22,26,30},{..., dimensions={0} | all-to-all | bytes 524288 | tf_op jit(solution)/shard_map/all_to_all | solution.py:354
  21.5 1.4 %collective-permute-start.2 = (bf16[8,4,16,256]{3,2,1,0:T(8,128)(2,1)S(1)}, bf16[8,4,16,256]{3,2,1,0:T(8,128)(2,1)S(1)}, u32[]{:S(2)}, u32[]{:S(2)}) collective-permute-start(bf16[8,4,16,256]{3,2,1,0:T(8,128)(2,1)S(1)} %all_to_all.5.own_ref), channel_id=1, source_target_pairs={{0,2},{1,3},{2,0},{3,1},{4,6},{5,7},{6,4},{7,5},{8,10},{9,11},{10,... | collective-permute-start | bytes 786440 | tf_op jit(solution)/shard_map/ppermute | solution.py:351
  23.0 0.0 collective-permute-start.1
  23.0 3.2 %collective-permute-start = (bf16[8,4,16,256]{3,2,1,0:T(8,128)(2,1)S(1)}, bf16[8,4,16,256]{3,2,1,0:T(8,128)(2,1)S(1)}, u32[]{:S(2)}, u32[]{:S(2)}) collective-permute-start(bf16[8,4,16,256]{3,2,1,0:T(8,128)(2,1)S(1)} %all_to_all.5.own_ref), channel_id=1, source_target_pairs={{0,1},{1,2},{2,3},{3,0},{4,5},{5,6},{6,7},{7,4},{8,9},{9,10},{10,1... | collective-permute-start | bytes 786440 | tf_op jit(solution)/shard_map/ppermute | solution.py:351
  26.2 6.3 %select.1.pack_hbm = bf16[2064,1024]{1,0:T(8,128)(2,1)} custom-call(s32[4]{0:T(128)} %bitcast.5, s32[4,256]{1,0:T(4,128)} %index_ref.1, bf16[4,256,256]{2,1,0:T(8,128)(2,1)} %cands_hbm.1, bf16[256,1024]{1,0:T(8,128)(2,1)} %wq_hbm.1, bf16[256,256]{1,0:T(8,128)(2,1)} %pre_wq_hbm.1, bf16[256,512]{1,0:T(8,128)(2,1)} %pre_wkv_hbm.1, bf16[256,2048]{1,0:T(8,128)(2,1)} %wkv_hbm.1, ...), custom_call_target="tpu_custom_call" | custom-call | flops 2000000000 | bytes 12582912 | tf_op jit(solution)/shard_map/select/pallas_call | solution.py:275
  32.5 1.6 %stage.1.fixed_ref = bf16[1040,1024]{1,0:T(8,128)(2,1)S(1)} custom-call(bf16[2064,1024]{1,0:T(8,128)(2,1)} %select.1.pack_hbm), custom_call_target="tpu_custom_call" | custom-call | bytes 4194304 | tf_op jit(solution)/shard_map/stage/pallas_call | solution.py:304
  34.2 0.0 collective-permute-done.2.c_ref
  34.2 0.8 %collective-permute-done.1.b_ref = bf16[8,4,16,256]{3,2,1,0:T(8,128)(2,1)S(1)} collective-permute-done((bf16[8,4,16,256]{3,2,1,0:T(8,128)(2,1)S(1)}, bf16[8,4,16,256]{3,2,1,0:T(8,128)(2,1)S(1)}, u32[]{:S(2)}, u32[]{:S(2)}) %collective-permute-start.1) | collective-permute-done | bytes 262176 | tf_op jit(solution)/shard_map/ppermute | solution.py:351
  34.9 0.0 collective-permute-done.a_ref
  34.9 18.8 %rank.1 = (f32[4,256]{1,0:T(4,128)}, f32[4,256]{1,0:T(4,128)}) custom-call(bf16[8,4,16,256]{3,2,1,0:T(8,128)(2,1)S(1)} %all_to_all.5.own_ref, bf16[8,4,16,256]{3,2,1,0:T(8,128)(2,1)S(1)} %collective-permute-done.a_ref, bf16[8,4,16,256]{3,2,1,0:T(8,128)(2,1)S(1)} %collective-permute-done.1.b_ref, bf16[8,4,16,256]{3,2,1,0:T(8,128)(2,1)S(1)} %collective-permute-done.2.c_ref, ...), custom_call_target="tpu_custom_call" | custom-call | flops 16000000000 | bytes 20971520 | tf_op jit(solution)/shard_map/rank/pallas_call | solution.py:323
Async XLA Ops:
  21.5 12.6 %collective-permute-start.2 = (bf16[8,4,16,256]{3,2,1,0:T(8,128)(2,1)S(1)}, bf16[8,4,16,256]{3,2,1,0:T(8,128)(2,1)S(1)}, u32[]{:S(2)}, u32[]{:S(2)}) collective-permute-start(bf16[8,4,16,256]{3,2,1,0:T(8,128)(2,1)S(1)} %all_to_all.5.own_ref), channel_id=1, source_target_pairs={{0,2},{1,3},{2,0},{3,1},{4,6},{5,7},{6,4},{7,5},{8,10},{9,11},{10,... | collective-permute-start | bytes 786440 | tf_op jit(solution)/shard_map/ppermute | solution.py:351
  23.0 12.0 %collective-permute-start.1 = (bf16[8,4,16,256]{3,2,1,0:T(8,128)(2,1)S(1)}, bf16[8,4,16,256]{3,2,1,0:T(8,128)(2,1)S(1)}, u32[]{:S(2)}, u32[]{:S(2)}) collective-permute-start(bf16[8,4,16,256]{3,2,1,0:T(8,128)(2,1)S(1)} %all_to_all.5.own_ref), channel_id=1, source_target_pairs={{0,3},{1,0},{2,1},{3,2},{4,7},{5,4},{6,5},{7,6},{8,11},{9,8},{10,9... | collective-permute-start | bytes 786440 | tf_op jit(solution)/shard_map/ppermute | solution.py:351
  23.0 12.0 %collective-permute-start = (bf16[8,4,16,256]{3,2,1,0:T(8,128)(2,1)S(1)}, bf16[8,4,16,256]{3,2,1,0:T(8,128)(2,1)S(1)}, u32[]{:S(2)}, u32[]{:S(2)}) collective-permute-start(bf16[8,4,16,256]{3,2,1,0:T(8,128)(2,1)S(1)} %all_to_all.5.own_ref), channel_id=1, source_target_pairs={{0,1},{1,2},{2,3},{3,0},{4,5},{5,6},{6,7},{7,4},{8,9},{9,10},{10,1... | collective-permute-start | bytes 786440 | tf_op jit(solution)/shard_map/ppermute | solution.py:351
where the time goes:
time: 54 us; the launch traced here: 53.9 us
  Pallas kernels  26.8 us (50%)
  blocking collectives  20.1 us (37%)
  starting transfers between devices  4.64 us (9%)
  between operations  0.82 us (2%)
  local copies, waits for them, and re-layouts  0.78 us (1%)
  waiting for transfers between devices  0.76 us (1%)
    all_to_all x1, blocking collectives, body(): lax.all_to_all(copies, 'cand', split_axis=0, concat_axis=0, tiled=True, a...  20.1 us
    pallas_call x1, Pallas kernels, rank_call(): pl.pallas_call(rank_kernel, name='rank', out_shape=(score, score), in_spe...  18.8 us
    pallas_call x1, Pallas kernels, select_call(): pl.pallas_call(select_kernel, name='select', out_shape=jax.ShapeDtypeStru...  6.34 us
    ppermute x3, starting transfers between devices, shift(): return lax.ppermute(x, 'cand', pairs)  4.64 us
    pallas_call x1, Pallas kernels, stage_call(): pl.pallas_call(stage_kernel, name='stage', out_shape=jax.ShapeDtypeStruct...  1.61 us
  transfers between devices with their start and end apart: 3, of which 1 were waited for; matrix products, arithmetic and copies ran while one was open for 0% of the time, Pallas kernels for 15%

commit v1 on v0

--- a/solution.py
+++ b/solution.py
@@ -15,7 +15,7 @@
 LOG2E = 1.4426950408889634
 GELU_A = math.sqrt(2.0 / math.pi)
 GELU_B = GELU_A * 0.044715
-ROW_TILES = (128, 176, 256)
+ROW_TILES = (128, 160, 176, 256)
 MLP_ROWS = (128, 192, 256, 352)
 MLP_COLS = 512
 PRE_Q = 1024

time: 54 us -> 55.2 us (1.022)
  the two profiles are of different devices: /device:TPU:30 before, /device:TPU:31 now
where the time goes in v1:
time: 55.2 us; the launch traced here: 54.3 us
  Pallas kernels  27.7 us (50%)
  blocking collectives  18.4 us (33%)
  starting transfers between devices  3.8 us (7%)
  waiting for transfers between devices  2.9 us (5%)
  between operations  0.82 us (1%)
  local copies, waits for them, and re-layouts  0.78 us (1%)
    pallas_call x1, Pallas kernels, rank_call(): pl.pallas_call(rank_kernel, name='rank', out_shape=(score, score), in_spe...  19.7 us
    all_to_all x1, blocking collectives, body(): lax.all_to_all(copies, 'cand', split_axis=0, concat_axis=0, tiled=True, a...  18.4 us
    pallas_call x1, Pallas kernels, select_call(): pl.pallas_call(select_kernel, name='select', out_shape=jax.ShapeDtypeStru...  6.34 us
    ppermute x3, starting transfers between devices, shift(): return lax.ppermute(x, 'cand', pairs)  3.8 us
    ppermute x3, waiting for transfers between devices, shift(): return lax.ppermute(x, 'cand', pairs)  2.9 us
    pallas_call x1, Pallas kernels, stage_call(): pl.pallas_call(stage_kernel, name='stage', out_shape=jax.ShapeDtypeStruct...  1.61 us
  transfers between devices with their start and end apart: 3, of which 1 were waited for; matrix products, arithmetic and copies ran while one was open for 0% of the time, Pallas kernels for 15%

profile of v1, /device:TPU:31, one launch (start us, length us, event | category | flops | bytes accessed | tf_op | source)
XLA Modules:
  0.0 54.3 jit_solution(15925437306892783917)
XLA Ops:
  0.6 0.8 %broadcast_in_dim.2 = bf16[8,4,16,256]{3,2,1,0:T(8,128)(2,1)S(1)} broadcast(bf16[4,16,256]{2,1,0:T(8,128)(2,1)} %param.11), dimensions={1,2,3} | broadcast | bytes 294912 | tf_op jit(solution)/shard_map/broadcast_in_dim | solution.py:353
  1.4 18.4 %all_to_all.5.own_ref = bf16[8,4,16,256]{3,2,1,0:T(8,128)(2,1)S(1)} all-to-all(bf16[8,4,16,256]{3,2,1,0:T(8,128)(2,1)S(1)} %broadcast_in_dim.2), channel_id=1, replica_groups={{0,4,8,12,16,20,24,28},{1,5,9,13,17,21,25,29},{2,6,10,14,18,22,26,30},{..., dimensions={0} | all-to-all | bytes 524288 | tf_op jit(solution)/shard_map/all_to_all | solution.py:354
  19.8 1.1 %collective-permute-start.2 = (bf16[8,4,16,256]{3,2,1,0:T(8,128)(2,1)S(1)}, bf16[8,4,16,256]{3,2,1,0:T(8,128)(2,1)S(1)}, u32[]{:S(2)}, u32[]{:S(2)}) collective-permute-start(bf16[8,4,16,256]{3,2,1,0:T(8,128)(2,1)S(1)} %all_to_all.5.own_ref), channel_id=1, source_target_pairs={{0,2},{1,3},{2,0},{3,1},{4,6},{5,7},{6,4},{7,5},{8,10},{9,11},{10,... | collective-permute-start | bytes 786440 | tf_op jit(solution)/shard_map/ppermute | solution.py:351
  20.9 0.0 collective-permute-start.1
  20.9 2.7 %collective-permute-start = (bf16[8,4,16,256]{3,2,1,0:T(8,128)(2,1)S(1)}, bf16[8,4,16,256]{3,2,1,0:T(8,128)(2,1)S(1)}, u32[]{:S(2)}, u32[]{:S(2)}) collective-permute-start(bf16[8,4,16,256]{3,2,1,0:T(8,128)(2,1)S(1)} %all_to_all.5.own_ref), channel_id=1, source_target_pairs={{0,1},{1,2},{2,3},{3,0},{4,5},{5,6},{6,7},{7,4},{8,9},{9,10},{10,1... | collective-permute-start | bytes 786440 | tf_op jit(solution)/shard_map/ppermute | solution.py:351
  23.6 6.3 %select.1.pack_hbm = bf16[2064,1024]{1,0:T(8,128)(2,1)} custom-call(s32[4]{0:T(128)} %bitcast.5, s32[4,256]{1,0:T(4,128)} %index_ref.1, bf16[4,256,256]{2,1,0:T(8,128)(2,1)} %cands_hbm.1, bf16[256,1024]{1,0:T(8,128)(2,1)} %wq_hbm.1, bf16[256,256]{1,0:T(8,128)(2,1)} %pre_wq_hbm.1, bf16[256,512]{1,0:T(8,128)(2,1)} %pre_wkv_hbm.1, bf16[256,2048]{1,0:T(8,128)(2,1)} %wkv_hbm.1, ...), custom_call_target="tpu_custom_call" | custom-call | flops 2000000000 | bytes 12582912 | tf_op jit(solution)/shard_map/select/pallas_call | solution.py:275
  29.9 1.6 %stage.1.fixed_ref = bf16[1040,1024]{1,0:T(8,128)(2,1)S(1)} custom-call(bf16[2064,1024]{1,0:T(8,128)(2,1)} %select.1.pack_hbm), custom_call_target="tpu_custom_call" | custom-call | bytes 4194304 | tf_op jit(solution)/shard_map/stage/pallas_call | solution.py:304
  31.5 0.0 collective-permute-done.2.c_ref
  31.5 2.9 %collective-permute-done.1.b_ref = bf16[8,4,16,256]{3,2,1,0:T(8,128)(2,1)S(1)} collective-permute-done((bf16[8,4,16,256]{3,2,1,0:T(8,128)(2,1)S(1)}, bf16[8,4,16,256]{3,2,1,0:T(8,128)(2,1)S(1)}, u32[]{:S(2)}, u32[]{:S(2)}) %collective-permute-start.1) | collective-permute-done | bytes 262176 | tf_op jit(solution)/shard_map/ppermute | solution.py:351
  34.4 0.0 collective-permute-done.a_ref
  34.4 19.7 %rank.1 = (f32[4,256]{1,0:T(4,128)}, f32[4,256]{1,0:T(4,128)}) custom-call(bf16[8,4,16,256]{3,2,1,0:T(8,128)(2,1)S(1)} %all_to_all.5.own_ref, bf16[8,4,16,256]{3,2,1,0:T(8,128)(2,1)S(1)} %collective-permute-done.a_ref, bf16[8,4,16,256]{3,2,1,0:T(8,128)(2,1)S(1)} %collective-permute-done.1.b_ref, bf16[8,4,16,256]{3,2,1,0:T(8,128)(2,1)S(1)} %collective-permute-done.2.c_ref, ...), custom_call_target="tpu_custom_call" | custom-call | flops 16000000000 | bytes 20971520 | tf_op jit(solution)/shard_map/rank/pallas_call | solution.py:323
Async XLA Ops:
  19.8 11.8 %collective-permute-start.2 = (bf16[8,4,16,256]{3,2,1,0:T(8,128)(2,1)S(1)}, bf16[8,4,16,256]{3,2,1,0:T(8,128)(2,1)S(1)}, u32[]{:S(2)}, u32[]{:S(2)}) collective-permute-start(bf16[8,4,16,256]{3,2,1,0:T(8,128)(2,1)S(1)} %all_to_all.5.own_ref), channel_id=1, source_target_pairs={{0,2},{1,3},{2,0},{3,1},{4,6},{5,7},{6,4},{7,5},{8,10},{9,11},{10,... | collective-permute-start | bytes 786440 | tf_op jit(solution)/shard_map/ppermute | solution.py:351
  20.9 13.6 %collective-permute-start.1 = (bf16[8,4,16,256]{3,2,1,0:T(8,128)(2,1)S(1)}, bf16[8,4,16,256]{3,2,1,0:T(8,128)(2,1)S(1)}, u32[]{:S(2)}, u32[]{:S(2)}) collective-permute-start(bf16[8,4,16,256]{3,2,1,0:T(8,128)(2,1)S(1)} %all_to_all.5.own_ref), channel_id=1, source_target_pairs={{0,3},{1,0},{2,1},{3,2},{4,7},{5,4},{6,5},{7,6},{8,11},{9,8},{10,9... | collective-permute-start | bytes 786440 | tf_op jit(solution)/shard_map/ppermute | solution.py:351
  20.9 13.6 %collective-permute-start = (bf16[8,4,16,256]{3,2,1,0:T(8,128)(2,1)S(1)}, bf16[8,4,16,256]{3,2,1,0:T(8,128)(2,1)S(1)}, u32[]{:S(2)}, u32[]{:S(2)}) collective-permute-start(bf16[8,4,16,256]{3,2,1,0:T(8,128)(2,1)S(1)} %all_to_all.5.own_ref), channel_id=1, source_target_pairs={{0,1},{1,2},{2,3},{3,0},{4,5},{5,6},{6,7},{7,4},{8,9},{9,10},{10,1... | collective-permute-start | bytes 786440 | tf_op jit(solution)/shard_map/ppermute | solution.py:351

commit v2 on v1

--- a/solution.py
+++ b/solution.py
@@ -15,7 +15,7 @@
 LOG2E = 1.4426950408889634
 GELU_A = math.sqrt(2.0 / math.pi)
 GELU_B = GELU_A * 0.044715
-ROW_TILES = (128, 160, 176, 256)
+ROW_TILES = (96, 128, 160, 176, 256)
 MLP_ROWS = (128, 192, 256, 352)
 MLP_COLS = 512
 PRE_Q = 1024

time: 55.2 us -> 54.4 us (0.986)
  the two profiles are of different devices: /device:TPU:31 before, /device:TPU:6 now
where the time goes in v2:
time: 54.4 us; the launch traced here: 53.8 us
  Pallas kernels  26.7 us (49%)
  blocking collectives  20.1 us (37%)
  starting transfers between devices  4.64 us (9%)
  between operations  0.82 us (2%)
  local copies, waits for them, and re-layouts  0.78 us (1%)
  waiting for transfers between devices  0.76 us (1%)
    all_to_all x1, blocking collectives, body(): lax.all_to_all(copies, 'cand', split_axis=0, concat_axis=0, tiled=True, a...  20.1 us
    pallas_call x1, Pallas kernels, rank_call(): pl.pallas_call(rank_kernel, name='rank', out_shape=(score, score), in_spe...  18.7 us
    pallas_call x1, Pallas kernels, select_call(): pl.pallas_call(select_kernel, name='select', out_shape=jax.ShapeDtypeStru...  6.35 us
    ppermute x3, starting transfers between devices, shift(): return lax.ppermute(x, 'cand', pairs)  4.64 us
    pallas_call x1, Pallas kernels, stage_call(): pl.pallas_call(stage_kernel, name='stage', out_shape=jax.ShapeDtypeStruct...  1.61 us
  transfers between devices with their start and end apart: 3, of which 1 were waited for; matrix products, arithmetic and copies ran while one was open for 0% of the time, Pallas kernels for 15%

profile of v2, /device:TPU:6, one launch (start us, length us, event | category | flops | bytes accessed | tf_op | source)
XLA Modules:
  0.0 53.8 jit_solution(12704866015310113042)
XLA Ops:
  0.6 0.8 %broadcast_in_dim.2 = bf16[8,4,16,256]{3,2,1,0:T(8,128)(2,1)S(1)} broadcast(bf16[4,16,256]{2,1,0:T(8,128)(2,1)} %param.11), dimensions={1,2,3} | broadcast | bytes 294912 | tf_op jit(solution)/shard_map/broadcast_in_dim | solution.py:353
  1.4 20.1 %all_to_all.5.own_ref = bf16[8,4,16,256]{3,2,1,0:T(8,128)(2,1)S(1)} all-to-all(bf16[8,4,16,256]{3,2,1,0:T(8,128)(2,1)S(1)} %broadcast_in_dim.2), channel_id=1, replica_groups={{0,4,8,12,16,20,24,28},{1,5,9,13,17,21,25,29},{2,6,10,14,18,22,26,30},{..., dimensions={0} | all-to-all | bytes 524288 | tf_op jit(solution)/shard_map/all_to_all | solution.py:354
  21.5 1.4 %collective-permute-start.2 = (bf16[8,4,16,256]{3,2,1,0:T(8,128)(2,1)S(1)}, bf16[8,4,16,256]{3,2,1,0:T(8,128)(2,1)S(1)}, u32[]{:S(2)}, u32[]{:S(2)}) collective-permute-start(bf16[8,4,16,256]{3,2,1,0:T(8,128)(2,1)S(1)} %all_to_all.5.own_ref), channel_id=1, source_target_pairs={{0,2},{1,3},{2,0},{3,1},{4,6},{5,7},{6,4},{7,5},{8,10},{9,11},{10,... | collective-permute-start | bytes 786440 | tf_op jit(solution)/shard_map/ppermute | solution.py:351
  23.0 0.0 collective-permute-start.1
  23.0 3.2 %collective-permute-start = (bf16[8,4,16,256]{3,2,1,0:T(8,128)(2,1)S(1)}, bf16[8,4,16,256]{3,2,1,0:T(8,128)(2,1)S(1)}, u32[]{:S(2)}, u32[]{:S(2)}) collective-permute-start(bf16[8,4,16,256]{3,2,1,0:T(8,128)(2,1)S(1)} %all_to_all.5.own_ref), channel_id=1, source_target_pairs={{0,1},{1,2},{2,3},{3,0},{4,5},{5,6},{6,7},{7,4},{8,9},{9,10},{10,1... | collective-permute-start | bytes 786440 | tf_op jit(solution)/shard_map/ppermute | solution.py:351
  26.2 6.3 %select.1.pack_hbm = bf16[2064,1024]{1,0:T(8,128)(2,1)} custom-call(s32[4]{0:T(128)} %bitcast.5, s32[4,256]{1,0:T(4,128)} %index_ref.1, bf16[4,256,256]{2,1,0:T(8,128)(2,1)} %cands_hbm.1, bf16[256,1024]{1,0:T(8,128)(2,1)} %wq_hbm.1, bf16[256,256]{1,0:T(8,128)(2,1)} %pre_wq_hbm.1, bf16[256,512]{1,0:T(8,128)(2,1)} %pre_wkv_hbm.1, bf16[256,2048]{1,0:T(8,128)(2,1)} %wkv_hbm.1, ...), custom_call_target="tpu_custom_call" | custom-call | flops 2000000000 | bytes 12582912 | tf_op jit(solution)/shard_map/select/pallas_call | solution.py:275
  32.5 1.6 %stage.1.fixed_ref = bf16[1040,1024]{1,0:T(8,128)(2,1)S(1)} custom-call(bf16[2064,1024]{1,0:T(8,128)(2,1)} %select.1.pack_hbm), custom_call_target="tpu_custom_call" | custom-call | bytes 4194304 | tf_op jit(solution)/shard_map/stage/pallas_call | solution.py:304
  34.2 0.0 collective-permute-done.2.c_ref
  34.2 0.8 %collective-permute-done.1.b_ref = bf16[8,4,16,256]{3,2,1,0:T(8,128)(2,1)S(1)} collective-permute-done((bf16[8,4,16,256]{3,2,1,0:T(8,128)(2,1)S(1)}, bf16[8,4,16,256]{3,2,1,0:T(8,128)(2,1)S(1)}, u32[]{:S(2)}, u32[]{:S(2)}) %collective-permute-start.1) | collective-permute-done | bytes 262176 | tf_op jit(solution)/shard_map/ppermute | solution.py:351
  34.9 0.0 collective-permute-done.a_ref
  34.9 18.7 %rank.1 = (f32[4,256]{1,0:T(4,128)}, f32[4,256]{1,0:T(4,128)}) custom-call(bf16[8,4,16,256]{3,2,1,0:T(8,128)(2,1)S(1)} %all_to_all.5.own_ref, bf16[8,4,16,256]{3,2,1,0:T(8,128)(2,1)S(1)} %collective-permute-done.a_ref, bf16[8,4,16,256]{3,2,1,0:T(8,128)(2,1)S(1)} %collective-permute-done.1.b_ref, bf16[8,4,16,256]{3,2,1,0:T(8,128)(2,1)S(1)} %collective-permute-done.2.c_ref, ...), custom_call_target="tpu_custom_call" | custom-call | flops 16000000000 | bytes 20971520 | tf_op jit(solution)/shard_map/rank/pallas_call | solution.py:323
Async XLA Ops:
  21.5 12.6 %collective-permute-start.2 = (bf16[8,4,16,256]{3,2,1,0:T(8,128)(2,1)S(1)}, bf16[8,4,16,256]{3,2,1,0:T(8,128)(2,1)S(1)}, u32[]{:S(2)}, u32[]{:S(2)}) collective-permute-start(bf16[8,4,16,256]{3,2,1,0:T(8,128)(2,1)S(1)} %all_to_all.5.own_ref), channel_id=1, source_target_pairs={{0,2},{1,3},{2,0},{3,1},{4,6},{5,7},{6,4},{7,5},{8,10},{9,11},{10,... | collective-permute-start | bytes 786440 | tf_op jit(solution)/shard_map/ppermute | solution.py:351
  23.0 12.0 %collective-permute-start.1 = (bf16[8,4,16,256]{3,2,1,0:T(8,128)(2,1)S(1)}, bf16[8,4,16,256]{3,2,1,0:T(8,128)(2,1)S(1)}, u32[]{:S(2)}, u32[]{:S(2)}) collective-permute-start(bf16[8,4,16,256]{3,2,1,0:T(8,128)(2,1)S(1)} %all_to_all.5.own_ref), channel_id=1, source_target_pairs={{0,3},{1,0},{2,1},{3,2},{4,7},{5,4},{6,5},{7,6},{8,11},{9,8},{10,9... | collective-permute-start | bytes 786440 | tf_op jit(solution)/shard_map/ppermute | solution.py:351
  23.0 12.0 %collective-permute-start = (bf16[8,4,16,256]{3,2,1,0:T(8,128)(2,1)S(1)}, bf16[8,4,16,256]{3,2,1,0:T(8,128)(2,1)S(1)}, u32[]{:S(2)}, u32[]{:S(2)}) collective-permute-start(bf16[8,4,16,256]{3,2,1,0:T(8,128)(2,1)S(1)} %all_to_all.5.own_ref), channel_id=1, source_target_pairs={{0,1},{1,2},{2,3},{3,0},{4,5},{5,6},{6,7},{7,4},{8,9},{9,10},{10,1... | collective-permute-start | bytes 786440 | tf_op jit(solution)/shard_map/ppermute | solution.py:351
